TPU v7x, 32 devices: a whole 2x2x4 slice. The times are simulated.
32 devices in a mesh: gx: 8 (over z, x), gy: 4 (over y, core).
Axes of the slice: x: 2, y: 2, z: 4, core: 2. Of those that a mesh axis runs over, the one named last changes fastest.
Arguments:
- field: bfloat16 [768, 128, 1536], P(None, 'gy', 'gx'), may hold values from -8 to 8
- norm_field: float32 [768, 128, 1536], P(('gx', 'gy')), may hold values from 0.5 to 2
- vertical: float32 [2, 64, 64], replicated, may hold values from -0.75 to 0.75
- x_filter: bfloat16 [1536, 1536], replicated, may hold values from -2 to 2
- y_filter: bfloat16 [768, 768], replicated, may hold values from -2 to 2
Outputs:
- covaried: bfloat16 [768, 128, 1536], P(None, 'gy', 'gx')
All inputs are finite; a program needn't handle non-finite values.
Results may differ from a plain program's by a relative error of at most 0.0075.
Values may be sent and summed in bfloat16 or wider, within the bound.
A program may use at most 128 MiB of HBM per device.

v0:
```python
import jax
import jax.numpy as jnp
from jax import lax
from jax.sharding import PartitionSpec as P


def xlines_forward(block, x_filter):
    width = x_filter.shape[0]
    result = jnp.dot(block.reshape(-1, width), x_filter, preferred_element_type=jnp.float32)
    return result.astype(jnp.bfloat16).reshape(block.shape)


def xlines_adjoint(block, x_filter):
    width = x_filter.shape[0]
    result = lax.dot_general(
        block.reshape(-1, width),
        x_filter,
        (((1,), (1,)), ((), ())),
        preferred_element_type=jnp.float32,
    )
    return result.astype(jnp.bfloat16).reshape(block.shape)


def columns_work(block, scales, vertical):
    species = vertical.shape[0]
    levels = vertical.shape[1]
    rows, comps, width = block.shape
    scaled = (scales * block.astype(jnp.float32)).reshape(rows, species, levels, width)
    lowered = jnp.einsum("slk,rslx->rskx", vertical, scaled, precision=lax.Precision.HIGHEST)
    raised = jnp.einsum("skl,rslx->rskx", vertical, lowered, precision=lax.Precision.HIGHEST)
    return (scales * raised.reshape(rows, comps, width)).astype(jnp.bfloat16)


def per_device(field, norm_field, vertical, x_filter, y_filter):
    lines, comps, width = field.shape
    first = lax.dot_general(
        y_filter,
        field.reshape(lines, comps * width),
        (((0,), (0,)), ((), ())),
        preferred_element_type=jnp.float32,
    )
    first = first.astype(jnp.bfloat16).reshape(lines, comps, width)
    xblock = lax.all_to_all(first, "gx", split_axis=0, concat_axis=2, tiled=True)
    second = xlines_forward(xblock, x_filter)
    columns = lax.all_to_all(second, "gy", split_axis=0, concat_axis=1, tiled=True)
    middle = columns_work(columns, norm_field, vertical)
    returned = lax.all_to_all(middle, "gy", split_axis=1, concat_axis=0, tiled=True)
    third = xlines_adjoint(returned, x_filter)
    ylines = lax.all_to_all(third, "gx", split_axis=2, concat_axis=0, tiled=True)
    result = jnp.dot(
        y_filter, ylines.reshape(lines, comps * width), preferred_element_type=jnp.float32
    )
    return result.astype(jnp.bfloat16).reshape(lines, comps, width)


def solution(mesh):
    return jax.shard_map(
        per_device,
        mesh=mesh,
        in_specs=(P(None, "gy", "gx"), P(("gx", "gy"), None, None), P(), P(), P()),
        out_specs=P(None, "gy", "gx"),
        check_vma=False,
    )
```

profile of v0, /device:TPU:30, one launch (start us, length us, event | category | flops | bytes accessed | tf_op | source)
XLA Modules:
  0.0 1088.9 jit_solution(4618035025842054751)
XLA Ops:
  0.0 0.0 copy-start
  0.0 1.3 copy-done
  1.3 13.5 %convolution_convert_fusion.3 = bf16[768,6144]{1,0:T(8,128)(2,1)} fusion(bf16[768,768]{1,0:T(8,128)(2,1)S(1)} %copy-done, bf16[768,6144]{0,1:T(8,128)(2,1)} %bitcast.69), kind=kOutput, calls=%fused_computation.11 | convolution fusion | flops 7252475904 | bytes 20054016 | tf_op jit(solution)/shard_map/dot_general | solution.py:36
  14.8 12.7 %copy.44 = bf16[768,6144]{0,1:T(8,128)(2,1)} copy(bf16[768,6144]{1,0:T(8,128)(2,1)} %convolution_convert_fusion.3) | data formatting | bytes 18874368 | tf_op jit(solution)/shard_map/convert_element_type | solution.py:42
  27.4 17.4 %copy.45 = bf16[768,32,192]{2,1,0:T(8,128)(2,1)} copy(bf16[768,32,192]{0,2,1:T(8,128)(2,1)} %bitcast.65) | data formatting | bytes 18874368 | tf_op jit(solution)/shard_map/reshape | solution.py:42
  44.9 276.5 %all_to_all.54 = bf16[768,32,192]{2,1,0:T(8,128)(2,1)S(1)} all-to-all(bf16[768,32,192]{2,1,0:T(8,128)(2,1)} %copy.45), channel_id=1, replica_groups=mesh['gx'=8,'gy'=4] {'gx'}, dimensions={0} | all-to-all | bytes 18874368 | tf_op jit(solution)/shard_map/all_to_all | solution.py:43
  321.4 10.7 copy.67
  332.1 19.9 %reshape.39 = bf16[3072,1536]{1,0:T(8,128)(2,1)} reshape(bf16[96,32,8,192]{3,2,1,0:T(8,128)(2,1)} %bitcast.62) | data formatting | bytes 18874368 | tf_op jit(solution)/shard_map/reshape | solution.py:9
  352.0 18.4 %convolution_convert_fusion.1 = bf16[3072,1536]{1,0:T(8,128)(2,1)S(1)} fusion(bf16[3072,1536]{1,0:T(8,128)(2,1)} %reshape.39, bf16[1536,1536]{1,0:T(8,128)(2,1)} %param.8), kind=kOutput, calls=%fused_computation.9 | convolution fusion | flops 14500233216 | bytes 23592960 | tf_op jit(solution)/shard_map/dot_general | solution.py:9
  370.4 107.2 %all_to_all.55 = bf16[96,32,1536]{2,1,0:T(8,128)(2,1)} all-to-all(bf16[96,32,1536]{2,1,0:T(8,128)(2,1)S(1)} %bitcast.66), channel_id=1, replica_groups=mesh['gx'=8,'gy'=4] {'gy'}, dimensions={0} | all-to-all | bytes 18874368 | tf_op jit(solution)/shard_map/all_to_all | solution.py:45
  477.6 13.0 %copy.47 = f32[4,24,32,1536]{3,2,0,1:T(8,128)} copy(bf16[4,24,32,1536]{3,2,1,0:T(8,128)(2,1)} %bitcast.63) | data formatting | bytes 28311552 | tf_op jit(solution)/shard_map/convert_element_type | solution.py:28
  490.6 0.0 copy-start.1
  490.6 20.2 %bitcast_multiply_fusion = f32[24,128,1536]{2,1,0:T(8,128)} fusion(f32[24,128,1536]{2,1,0:T(8,128)} %param.6, f32[4,24,32,1536]{3,2,0,1:T(8,128)} %copy.47), kind=kLoop, calls=%fused_computation | loop fusion | flops 4718592 | bytes 56623104 | tf_op jit(solution)/shard_map/mul | solution.py:28
  510.8 0.0 copy-done.1
  510.8 22.3 %fusion.3 = f32[2,24,1536,64]{2,3,1,0:T(8,128)S(1)} fusion(f32[24,2,64,1536]{3,2,1,0:T(8,128)} %bitcast.59, f32[2,64,64]{2,1,0:T(8,128)S(1)} %copy-done.1), kind=kOutput, calls=%fused_computation.5 | convolution fusion | flops 3623878656 | bytes 37781504 | tf_op jit(solution)/shard_map/slk,rslx->rskx/dot_general | solution.py:29
  533.1 22.8 %fusion.5 = f32[24,2,64,1536]{3,2,0,1:T(8,128)} fusion(f32[2,24,1536,64]{2,3,1,0:T(8,128)S(1)} %fusion.3, f32[2,64,64]{2,1,0:T(8,128)S(1)} %copy-done.1), kind=kOutput, calls=%fused_computation.12 | convolution fusion | flops 3623878656 | bytes 37781504 | tf_op jit(solution)/shard_map/skl,rslx->rskx/dot_general | solution.py:30
  556.0 7.0 copy.50
  563.0 12.4 %fusion = bf16[24,128,1536]{2,1,0:T(8,128)(2,1)} fusion(f32[24,128,1536]{2,1,0:T(8,128)} %param.6, f32[24,2,64,1536]{3,2,1,0:T(8,128)S(1)} %copy.50), kind=kLoop, calls=%fused_computation.2 | loop fusion | flops 9437184 | bytes 47185920 | tf_op jit(solution)/shard_map/convert_element_type | solution.py:31
  575.4 12.5 %copy.51 = bf16[24,128,1536]{2,0,1:T(8,128)(2,1)} copy(bf16[24,128,1536]{2,1,0:T(8,128)(2,1)} %fusion) | data formatting | bytes 18874368 | tf_op jit(solution)/shard_map/convert_element_type | solution.py:31
  587.9 112.6 %all_to_all.56 = bf16[24,128,1536]{2,0,1:T(8,128)(2,1)} all-to-all(bf16[24,128,1536]{2,0,1:T(8,128)(2,1)} %copy.51), channel_id=1, replica_groups=mesh['gx'=8,'gy'=4] {'gy'}, dimensions={1} | all-to-all | bytes 18874368 | tf_op jit(solution)/shard_map/all_to_all | solution.py:47
  700.5 10.8 copy.53
  711.3 20.2 %convolution_convert_fusion = bf16[3072,1536]{1,0:T(8,128)(2,1)} fusion(bf16[3072,1536]{1,0:T(8,128)(2,1)} %bitcast.67, bf16[1536,1536]{1,0:T(8,128)(2,1)} %param.8), kind=kOutput, calls=%fused_computation.8 | convolution fusion | flops 14500233216 | bytes 23592960 | tf_op jit(solution)/shard_map/dot_general | solution.py:15
  731.5 17.4 %copy.54 = bf16[96,32,1536]{0,1,2:T(8,128)(2,1)} copy(bf16[96,32,1536]{2,1,0:T(8,128)(2,1)} %bitcast.68) | data formatting | bytes 18874368 | tf_op jit(solution)/shard_map/reshape | solution.py:21
  748.8 280.3 %all_to_all.57 = bf16[96,32,1536]{0,1,2:T(8,128)(2,1)} all-to-all(bf16[96,32,1536]{0,1,2:T(8,128)(2,1)} %copy.54), channel_id=1, replica_groups=mesh['gx'=8,'gy'=4] {'gx'}, dimensions={2} | all-to-all | bytes 18874368 | tf_op jit(solution)/shard_map/all_to_all | solution.py:49
  1029.2 25.6 %copy.56 = bf16[8,96,32,192]{3,2,1,0:T(8,128)(2,1)} copy(bf16[8,96,32,192]{1,2,3,0:T(8,128)(2,1)} %bitcast.61) | data formatting | bytes 18874368 | tf_op jit(solution)/shard_map/all_to_all | solution.py:49
  1054.7 20.2 %reshape.45 = bf16[768,6144]{1,0:T(8,128)(2,1)} reshape(bf16[8,96,32,192]{3,2,1,0:T(8,128)(2,1)} %copy.56) | data formatting | bytes 18874368 | tf_op jit(solution)/shard_map/reshape | solution.py:51
  1074.9 13.5 %convolution_convert_fusion.2 = bf16[6144,768]{1,0:T(8,128)(2,1)} fusion(bf16[768,6144]{1,0:T(8,128)(2,1)} %reshape.45, bf16[768,768]{1,0:T(8,128)(2,1)S(1)} %copy-done), kind=kOutput, calls=%fused_computation.10 | convolution fusion | flops 7252475904 | bytes 20054016 | tf_op jit(solution)/shard_map/dot_general | solution.py:50
Async XLA Ops:
  0.0 1.3 copy-start
  490.6 20.2 %copy-start.1 = (f32[2,64,64]{2,1,0:T(8,128)S(1)}, f32[2,64,64]{2,1,0:T(8,128)}, u32[]{:S(2)}) copy-start(f32[2,64,64]{2,1,0:T(8,128)} %param.7) | copy-start | bytes 98308
where the time goes:
time: 1100 us; the launch traced here: 1090 us
  blocking collectives  777 us (71%)
  local copies, waits for them, and re-layouts  168 us (15%)
  matrix products  111 us (10%)
  other arithmetic  32.6 us (3%)
    all_to_all x1, blocking collectives, per_device(): lax.all_to_all(third, 'gx', split_axis=2, concat_axis=0, tiled=True)  280 us
    all_to_all x1, blocking collectives, per_device(): lax.all_to_all(first, 'gx', split_axis=0, concat_axis=2, tiled=True)  277 us
    all_to_all x1, blocking collectives, per_device(): lax.all_to_all(middle, 'gy', split_axis=1, concat_axis=0, tiled=True)  113 us
    all_to_all x1, blocking collectives, per_device(): lax.all_to_all(second, 'gy', split_axis=0, concat_axis=1, tiled=True)  107 us
    all_to_all x1, local copies, waits for them, and re-layouts, per_device(): lax.all_to_all(third, 'gx', split_axis=2, concat_axis=0, tiled=True)  25.6 us
    dot_general x1, matrix products, columns_work(): jnp.einsum('skl,rslx->rskx', vertical, lowered, precision=lax.Precision.H...  22.8 us
    dot_general x1, matrix products, columns_work(): jnp.einsum('slk,rslx->rskx', vertical, scaled, precision=lax.Precision.HI...  22.3 us

commit v1 on v0

--- a/solution.py
+++ b/solution.py
@@ -1,7 +1,17 @@
+import functools
+
 import jax
 import jax.numpy as jnp
 from jax import lax
+from jax.experimental import pallas as pl
+from jax.experimental.pallas import tpu as pltpu
 from jax.sharding import PartitionSpec as P
+
+MESH = pl.DeviceIdType.MESH
+LANES = 128
+HALF = 64
+CHUNK_ROWS = 8
+TILE = 256
 
 
 def xlines_forward(block, x_filter):
@@ -31,7 +41,7 @@
     return (scales * raised.reshape(rows, comps, width)).astype(jnp.bfloat16)
 
 
-def per_device(field, norm_field, vertical, x_filter, y_filter):
+def general_plan(field, norm_field, vertical, x_filter, y_filter):
     lines, comps, width = field.shape
     first = lax.dot_general(
         y_filter,
@@ -53,9 +63,308 @@
     return result.astype(jnp.bfloat16).reshape(lines, comps, width)
 
 
+def exchange_kernel(
+    gx, gy, first, norm, xf, factor, ylines,
+    xb, sec, col, ret, xs, nbuf,
+    b_send, b_recv, d_send, d_recv, e_send, e_recv, f_send, f_recv, own, nsem,
+):
+    chunks, _, rows, _, comps_half, _ = xb.shape
+    comps = 2 * comps_half
+    width = xf.shape[1]
+    species, levels, _ = factor.shape
+    me_x = lax.axis_index("gx")
+    me_y = lax.axis_index("gy")
+    whole_a = gx * LANES
+    part_b = gx * HALF
+    m = rows * comps_half
+
+    barrier = pltpu.get_barrier_semaphore()
+    for s in range(1, gx):
+        pl.semaphore_signal(
+            barrier, inc=1, device_id={"gx": lax.rem(me_x + s, gx)}, device_id_type=MESH)
+    for s in range(1, gy):
+        pl.semaphore_signal(
+            barrier, inc=1, device_id={"gy": lax.rem(me_y + s, gy)}, device_id_type=MESH)
+    pl.semaphore_wait(barrier, gx + gy - 2)
+
+    def remote(src, dst, send, recv, axis, peer):
+        return pltpu.make_async_remote_copy(
+            src_ref=src, dst_ref=dst, send_sem=send, recv_sem=recv,
+            device_id={axis: peer}, device_id_type=MESH)
+
+    def out_x(j):
+        copies = []
+        for s in range(1, gx):
+            peer = lax.rem(me_x + s, gx)
+            copies.append(remote(first.at[j, peer], xb.at[j, me_x],
+                                 b_send.at[j, s - 1], b_recv.at[j, s - 1], "gx", peer))
+        mine = pltpu.make_async_copy(first.at[j, me_x], xb.at[j, me_x], own.at[0, j])
+        return copies, mine
+
+    def out_y(j):
+        copies = []
+        for s in range(1, gy):
+            peer = lax.rem(me_y + s, gy)
+            copies.append(remote(
+                sec.at[j, pl.ds(peer * CHUNK_ROWS, CHUNK_ROWS)],
+                col.at[j, :, pl.ds(pl.multiple_of(me_y * comps, comps), comps), :],
+                d_send.at[j, s - 1], d_recv.at[j, s - 1], "gy", peer))
+        mine = pltpu.make_async_copy(
+            sec.at[j, pl.ds(me_y * CHUNK_ROWS, CHUNK_ROWS)],
+            col.at[j, :, pl.ds(pl.multiple_of(me_y * comps, comps), comps), :], own.at[1, j])
+        return copies, mine
+
+    def back_y(j):
+        copies = []
+        for s in range(1, gy):
+            peer = lax.rem(me_y + s, gy)
+            copies.append(remote(
+                col.at[j, :, pl.ds(pl.multiple_of(peer * comps, comps), comps), :],
+                ret.at[j, pl.ds(me_y * CHUNK_ROWS, CHUNK_ROWS)],
+                e_send.at[j, s - 1], e_recv.at[j, s - 1], "gy", peer))
+        mine = pltpu.make_async_copy(
+            col.at[j, :, pl.ds(pl.multiple_of(me_y * comps, comps), comps), :],
+            ret.at[j, pl.ds(me_y * CHUNK_ROWS, CHUNK_ROWS)], own.at[2, j])
+        return copies, mine
+
+    def back_x(j):
+        copies = []
+        for s in range(1, gx):
+            peer = lax.rem(me_x + s, gx)
+            copies.append(remote(xb.at[j, peer], ylines.at[j, me_x],
+                                 f_send.at[j, s - 1], f_recv.at[j, s - 1], "gx", peer))
+        mine = pltpu.make_async_copy(xb.at[j, me_x], ylines.at[j, me_x], own.at[3, j])
+        return copies, mine
+
+    def start(pair):
+        for copy in pair[0]:
+            copy.start()
+        pair[1].start()
+        return pair
+
+    def arrive(pair):
+        for copy in pair[0]:
+            copy.wait_recv()
+        pair[1].wait()
+
+    def drain(pair):
+        for copy in pair[0]:
+            copy.wait_send()
+
+    def norm_load(j):
+        return pltpu.make_async_copy(norm.at[pl.ds(j * CHUNK_ROWS, CHUNK_ROWS)], nbuf, nsem)
+
+    def low_lanes(shape):
+        return lax.broadcasted_iota(jnp.int32, shape, len(shape) - 1) < HALF
+
+    def forward(j):
+        for h in range(2):
+            for g in range(gx):
+                xs[:, g * LANES:(g + 1) * LANES] = xb[j, g, :, h].reshape(m, LANES)
+            for q in range(gx // 2):
+                even = xb[j, 2 * q, :, 2].reshape(m, LANES)
+                odd = xb[j, 2 * q + 1, :, 2].reshape(m, LANES)
+                low, high = (even, odd) if h == 0 else (odd, even)
+                at = whole_a + q * LANES
+                xs[:, at:at + LANES] = jnp.where(low_lanes((m, LANES)), low, high)
+            base = whole_a + part_b * h
+
+            @pl.loop(0, width // TILE)
+            def _(n):
+                cols = pl.ds(pl.multiple_of(n * TILE, TILE), TILE)
+                acc = jnp.dot(xs[:, :whole_a], xf[:whole_a, cols],
+                              preferred_element_type=jnp.float32)
+                acc += jnp.dot(xs[:, whole_a:], xf[base:base + part_b, cols],
+                               preferred_element_type=jnp.float32)
+                sec[j, :, h * comps_half:(h + 1) * comps_half, cols] = (
+                    acc.astype(jnp.bfloat16).reshape(rows, comps_half, TILE))
+
+    def columns(j):
+        @pl.loop(0, CHUNK_ROWS)
+        def _(r):
+            for s in range(species):
+                here = slice(s * levels, (s + 1) * levels)
+                for n in range(0, width, 2 * TILE):
+                    lanes = slice(n, n + 2 * TILE)
+                    scales = nbuf[r, here, lanes]
+                    scaled = scales * col[j, r, here, lanes].astype(jnp.float32)
+                    high = scaled.astype(jnp.bfloat16)
+                    low = (scaled - high.astype(jnp.float32)).astype(jnp.bfloat16)
+                    stack = jnp.concatenate([high, high, low], axis=0)
+                    raised = jnp.dot(factor[s], stack, preferred_element_type=jnp.float32)
+                    col[j, r, here, lanes] = (scales * raised).astype(jnp.bfloat16)
+
+    def adjoint(j):
+        def lines(h):
+            return ret[j, :, h * comps_half:(h + 1) * comps_half, :].reshape(m, width)
+
+        def dots(block, at):
+            return lax.dot_general(block, xf[pl.ds(at, TILE), :], (((1,), (1,)), ((), ())),
+                                   preferred_element_type=jnp.float32)
+
+        for h in range(2):
+            @pl.loop(0, whole_a // TILE)
+            def _(n):
+                part = dots(lines(h), pl.multiple_of(n * TILE, TILE))
+                for i in range(TILE // LANES):
+                    xb[j, n * (TILE // LANES) + i, :, h] = (
+                        part[:, i * LANES:(i + 1) * LANES].astype(jnp.bfloat16)
+                        .reshape(rows, comps_half, LANES))
+
+        @pl.loop(0, part_b // TILE)
+        def _(n):
+            at = pl.multiple_of(whole_a + n * TILE, TILE)
+            part0 = dots(lines(0), at)
+            part1 = dots(lines(1), pl.multiple_of(at + part_b, TILE))
+            for i in range(TILE // LANES):
+                p0 = part0[:, i * LANES:(i + 1) * LANES]
+                p1 = part1[:, i * LANES:(i + 1) * LANES]
+                mask = low_lanes((m, LANES))
+                g = 2 * (n * (TILE // LANES) + i)
+                xb[j, g, :, 2] = jnp.where(mask, p0, p1).astype(jnp.bfloat16).reshape(
+                    rows, comps_half, LANES)
+                xb[j, g + 1, :, 2] = jnp.where(mask, p1, p0).astype(jnp.bfloat16).reshape(
+                    rows, comps_half, LANES)
+
+    bs, ds, es, fs = {}, {}, {}, {}
+
+    def stage_c(j):
+        arrive(bs[j])
+        if j + 2 < chunks:
+            bs[j + 2] = start(out_x(j + 2))
+        forward(j)
+        ds[j] = start(out_y(j))
+
+    def stage_e(j):
+        arrive(ds[j])
+        norm_load(j).wait()
+        columns(j)
+        es[j] = start(back_y(j))
+        if j + 1 < chunks:
+            norm_load(j + 1).start()
+
+    def stage_f(j):
+        arrive(es[j])
+        adjoint(j)
+        fs[j] = start(back_x(j))
+
+    norm_load(0).start()
+    for j in range(min(2, chunks)):
+        bs[j] = start(out_x(j))
+    stage_c(0)
+    stage_e(0)
+    for j in range(1, chunks):
+        stage_c(j)
+        stage_f(j - 1)
+        stage_e(j)
+    stage_f(chunks - 1)
+    for j in range(chunks):
+        arrive(fs[j])
+    for j in range(chunks):
+        for pair in (bs[j], ds[j], es[j], fs[j]):
+            drain(pair)
+
+
+def exchange(gx, gy, first, norm_field, xf, factor):
+    chunks, _, rows, _, comps_half, _ = first.shape
+    width = xf.shape[1]
+    dma = pltpu.SemaphoreType.DMA
+    all_comps = norm_field.shape[1]
+    return pl.pallas_call(
+        functools.partial(exchange_kernel, gx, gy),
+        out_shape=jax.ShapeDtypeStruct(first.shape, jnp.bfloat16),
+        in_specs=[
+            pl.BlockSpec(memory_space=pl.ANY),
+            pl.BlockSpec(memory_space=pl.ANY),
+            pl.BlockSpec(memory_space=pltpu.VMEM),
+            pl.BlockSpec(memory_space=pltpu.VMEM),
+        ],
+        out_specs=pl.BlockSpec(memory_space=pl.ANY),
+        scratch_shapes=[
+            pltpu.VMEM(first.shape, jnp.bfloat16),
+            pltpu.VMEM((chunks, rows, 2 * comps_half, width), jnp.bfloat16),
+            pltpu.VMEM((chunks, CHUNK_ROWS, all_comps, width), jnp.bfloat16),
+            pltpu.VMEM((chunks, rows, 2 * comps_half, width), jnp.bfloat16),
+            pltpu.VMEM((rows * comps_half, width), jnp.bfloat16),
+            pltpu.VMEM((CHUNK_ROWS, all_comps, width), jnp.float32),
+            dma((chunks, gx - 1)), dma((chunks, gx - 1)),
+            dma((chunks, gy - 1)), dma((chunks, gy - 1)),
+            dma((chunks, gy - 1)), dma((chunks, gy - 1)),
+            dma((chunks, gx - 1)), dma((chunks, gx - 1)),
+            dma((4, chunks)), dma,
+        ],
+        compiler_params=pltpu.CompilerParams(
+            collective_id=0, has_side_effects=True, vmem_limit_bytes=60 * 1024 * 1024),
+        name="exchange",
+    )(first, norm_field, xf, factor)
+
+
+def pack(block, odd):
+    half = block.shape[1] // 2
+    b0, b1 = block[:, :half, LANES:], block[:, half:, LANES:]
+    tail = jnp.where(odd, jnp.concatenate([b1, b0], 2), jnp.concatenate([b0, b1], 2))
+    return jnp.concatenate([block[:, :half, :LANES], block[:, half:, :LANES], tail], 1)
+
+
+def unpack(block, odd):
+    half = block.shape[1] // 3
+    tail = block[:, 2 * half:]
+    low, high = tail[:, :, :HALF], tail[:, :, HALF:]
+    b0, b1 = jnp.where(odd, high, low), jnp.where(odd, low, high)
+    return jnp.concatenate([
+        jnp.concatenate([block[:, :half], b0], 2),
+        jnp.concatenate([block[:, half:2 * half], b1], 2)], 1)
+
+
+def fused_plan(gx, gy, field, norm_field, vertical, x_filter, y_filter):
+    lines, comps, width = field.shape
+    chunks = norm_field.shape[0] // CHUNK_ROWS
+    half = comps // 2
+    odd = lax.rem(lax.axis_index("gx"), 2) == 1
+
+    product = jnp.einsum("skl,sml->skm", vertical, vertical, precision=lax.Precision.HIGHEST)
+    high = lax.reduce_precision(product, 8, 7)
+    low = product - high
+    factor = jnp.concatenate([high, low, high], 2).astype(jnp.bfloat16)
+
+    strips = x_filter.reshape(gx, width, -1)
+    tails = strips[:, LANES:].reshape(gx // 2, 2, HALF, -1)
+    xf = jnp.concatenate([
+        strips[:, :LANES].reshape(gx * LANES, -1),
+        tails.reshape(gx * HALF, -1),
+        tails[:, ::-1].reshape(gx * HALF, -1)], 0)
+
+    yf = y_filter.reshape(lines, gx, gy, chunks, CHUNK_ROWS)
+    yf = yf.transpose(0, 3, 1, 2, 4).reshape(lines, lines)
+
+    packed = pack(field, odd)
+    first = lax.dot_general(
+        yf, packed, (((0,), (0,)), ((), ())), preferred_element_type=jnp.float32)
+    first = first.astype(jnp.bfloat16).reshape(
+        chunks, gx, gy * CHUNK_ROWS, 3, half, LANES)
+    ylines = exchange(gx, gy, first, norm_field, xf, factor)
+    ylines = ylines.reshape(lines, 3 * half, LANES)
+    result = lax.dot_general(
+        yf, ylines, (((1,), (0,)), ((), ())), preferred_element_type=jnp.float32)
+    return unpack(result.astype(jnp.bfloat16), odd)
+
+
+def per_device(gx, gy, field, norm_field, vertical, x_filter, y_filter):
+    lines, comps, width = field.shape
+    rows, all_comps, whole = norm_field.shape
+    fits = (
+        width == LANES + HALF and comps == 32 and rows % CHUNK_ROWS == 0 and gx % 4 == 0
+        and gy > 1 and whole % (2 * TILE) == 0 and vertical.shape[1] % 16 == 0
+        and rows * all_comps * whole <= 24 * 128 * 1536
+    )
+    if fits:
+        return fused_plan(gx, gy, field, norm_field, vertical, x_filter, y_filter)
+    return general_plan(field, norm_field, vertical, x_filter, y_filter)
+
+
 def solution(mesh):
     return jax.shard_map(
-        per_device,
+        functools.partial(per_device, mesh.shape["gx"], mesh.shape["gy"]),
         mesh=mesh,
         in_specs=(P(None, "gy", "gx"), P(("gx", "gy"), None, None), P(), P(), P()),
         out_specs=P(None, "gy", "gx"),

time: 1100 us -> 496 us (0.45)
  blocking collectives: 777 us -> 0 us
  Pallas kernels: 0 us -> 419 us
  local copies, waits for them, and re-layouts: 168 us -> 26.4 us
  matrix products: 111 us -> 28.5 us
    all_to_all x4 -> x0, blocking collectives: 777 us -> none  [the longest x1 280 us: per_device(): lax.all_to_all(third, 'gx', split_axis=2, concat_axis=0, tiled=True)]
    pallas_call x0 -> x1, Pallas kernels: none -> 419 us  [exchange(): pl.pallas_call(functools.partial(exchange_kernel, gx, gy), out_shape=jax....]
    dot_general x6 -> x3, matrix products: 111 us -> 28.5 us  [the longest x1 17.1 us: fused_plan(): lax.dot_general(yf, ylines, (((1,), (0,)), ((), ())), preferred_element_t...]
    reshape x4 -> x0, local copies, waits for them, and re-layouts: 74.8 us -> none  [the longest x1 20.2 us: per_device(): ylines.reshape(lines, comps * width)]
    all_to_all x3 -> x0, local copies, waits for them, and re-layouts: 47 us -> none  [the longest x1 25.6 us: per_device(): lax.all_to_all(third, 'gx', split_axis=2, concat_axis=0, tiled=True)]
    convert_element_type x3 -> x1, local copies, waits for them, and re-layouts: 38.2 us -> 13.2 us  [fused_plan(): first.astype(jnp.bfloat16)]
    concatenate x0 -> x3, other arithmetic: none -> 20.6 us  [the longest x1 16.8 us: unpack(): jnp.concatenate([jnp.concatenate([block[:, :half], b0], 2), jnp.concatena...]
    mul x1 -> x0, other arithmetic: 20.2 us -> none  [columns_work(): scales * block.astype(jnp.float32)]
where the time goes in v1:
time: 496 us
  Pallas kernels  419 us (84%)
  matrix products  28.5 us (6%)
  local copies, waits for them, and re-layouts  26.4 us (5%)
  other arithmetic  21.7 us (4%)
    pallas_call x1, Pallas kernels, exchange(): pl.pallas_call(functools.partial(exchange_kernel, gx, gy), out_shape=jax....  419 us
    dot_general x1, matrix products, fused_plan(): lax.dot_general(yf, ylines, (((1,), (0,)), ((), ())), preferred_element_t...  17.1 us
    concatenate x1, other arithmetic, unpack(): jnp.concatenate([jnp.concatenate([block[:, :half], b0], 2), jnp.concatena...  16.8 us
    convert_element_type x1, local copies, waits for them, and re-layouts, fused_plan(): first.astype(jnp.bfloat16)  13.2 us
    dot_general x1, matrix products, fused_plan(): lax.dot_general(yf, packed, (((0,), (0,)), ((), ())), preferred_element_t...  11.2 us

profile of v1, /device:TPU:30, one launch (start us, length us, event | category | flops | bytes accessed | tf_op | source)
XLA Modules:
  0.0 495.6 jit_solution(2716886179780766039)
XLA Ops:
  0.0 0.0 copy-start
  0.0 0.8 copy-done
  0.8 0.2 fusion.10
  1.1 0.7 pad_maximum_fusion.1.factor
  1.8 1.6 copy.9
  3.4 1.2 copy.10
  4.5 1.6 slice.42
  6.1 0.1 rev.3
  6.2 2.1 slice.41
  8.3 3.1 pad_maximum_fusion.xf
  11.4 2.1 fusion.13
  13.5 0.9 maximum_select_fusion
  14.4 0.0 slice-start
  14.4 0.0 copy-start.2
  14.4 2.8 slice-done
  17.2 0.3 copy-done.2
  17.5 11.2 %convert_bitcast_fusion.1 = bf16[768,48,128]{0,2,1:T(8,128)(2,1)} fusion(bf16[768,768,1]{0,1,2:T(8,128)(2,1)S(1)} %bitcast.31, bf16[768,16,128]{0,2,1:T(8,128)(2,1)S(1)} %maximum_select_fusion, bf16[768,32,128]{0,2,1:T(8,128)(2,1)S(1)} %slice-done), kind=kOutput, calls=%fused_computation.8 | convolution fusion | flops 7257194496 | bytes 20054016 | tf_op jit(solution)/shard_map/dot_general | solution.py:341
  28.7 13.2 %copy.12 = bf16[768,48,128]{2,1,0:T(8,128)(2,1)} copy(bf16[768,48,128]{0,2,1:T(8,128)(2,1)} %convert_bitcast_fusion.1) | data formatting | bytes 18874368 | tf_op jit(solution)/shard_map/convert_element_type | solution.py:343
  41.9 418.9 %exchange.1 = bf16[3,8,32,3,16,128]{5,4,3,2,1,0:T(8,128)(2,1)} custom-call(bf16[3,8,32,3,16,128]{5,4,3,2,1,0:T(8,128)(2,1)} %bitcast.22, f32[24,128,1536]{2,1,0:T(8,128)} %norm.1, bf16[2048,1536]{1,0:T(8,128)(2,1)} %pad_maximum_fusion.xf, bf16[2,64,192]{2,1,0:T(8,128)(2,1)} %pad_maximum_fusion.1.factor), custom_call_target="tpu_custom_call" | custom-call | tf_op jit(solution)/shard_map/exchange/pallas_call | solution.py:273
  460.8 17.1 %convert_bitcast_fusion = bf16[768,48,128]{0,2,1:T(8,128)(2,1)S(1)} fusion(bf16[768,768,1]{0,1,2:T(8,128)(2,1)S(1)} %bitcast.32, bf16[768,48,128]{2,1,0:T(8,128)(2,1)} %bitcast.26), kind=kOutput, calls=%fused_computation.7 | convolution fusion | flops 7252475904 | bytes 20054016 | tf_op jit(solution)/shard_map/dot_general | solution.py:347
  477.9 0.2 broadcast_select_fusion.1
  478.1 0.6 fusion.12
  478.8 0.0 copy-start.1
  478.8 16.8 %maximum_maximum_fusion = bf16[768,32,192]{0,2,1:T(8,128)(2,1)} fusion(bf16[768,16,64]{0,2,1:T(8,128)(2,1)S(1)} %get-tuple-element.8, bf16[768,16,128]{0,2,1:T(8,128)(2,1)S(1)} %get-tuple-element.6, bf16[768,16,64]{0,2,1:T(8,128)(2,1)S(1)} %get-tuple-element.7, bf16[768,16,128]{0,2,1:T(8,128)(2,1)S(1)} %get-tuple-element.5), kind=kLoop, calls=%fused_computation.4 | loop fusion | flops 37748736 | bytes 18874368 | tf_op jit(solution)/shard_map/concatenate | solution.py:314
  495.6 0.0 copy-done.1
Async XLA Ops:
  0.0 0.8 copy-start
  14.4 2.8 slice-start
  14.4 3.1 copy-start.2
  478.8 16.9 %copy-start.1 = (f32[2,64,64]{2,1,0:T(8,128)S(1)}, f32[2,64,64]{2,1,0:T(8,128)}, u32[]{:S(2)}) copy-start(f32[2,64,64]{2,1,0:T(8,128)} %param.7) | copy-start | bytes 98308

commit v2 on v1

--- a/solution.py
+++ b/solution.py
@@ -64,11 +64,11 @@
 
 
 def exchange_kernel(
-    gx, gy, first, norm, xf, factor, ylines,
-    xb, sec, col, ret, xs, nbuf,
-    b_send, b_recv, d_send, d_recv, e_send, e_recv, f_send, f_recv, own, nsem,
+    gx, gy, first, norm, x_filter, factor, ylines,
+    xb, sec, col, ret, xs, nbuf, xf, spread,
+    b_send, b_recv, d_send, d_recv, e_send, e_recv, f_send, f_recv, own, nsem, xsem,
 ):
-    chunks, _, rows, _, comps_half, _ = xb.shape
+    chunks, _, _, comps_half, rows, _ = xb.shape
     comps = 2 * comps_half
     width = xf.shape[1]
     species, levels, _ = factor.shape
@@ -78,6 +78,18 @@
     part_b = gx * HALF
     m = rows * comps_half
 
+    strip = LANES + HALF
+    xf_copies = []
+    for g in range(gx):
+        tail = x_filter.at[pl.ds(g * strip + LANES, HALF)]
+        for src, at in (
+            (x_filter.at[pl.ds(g * strip, LANES)], g * LANES),
+            (tail, whole_a + g * HALF),
+            (tail, whole_a + part_b + (g ^ 1) * HALF),
+        ):
+            xf_copies.append(pltpu.make_async_copy(
+                src, xf.at[pl.ds(at, src.shape[0])], xsem.at[len(xf_copies)]))
+
     barrier = pltpu.get_barrier_semaphore()
     for s in range(1, gx):
         pl.semaphore_signal(
@@ -92,13 +104,16 @@
             src_ref=src, dst_ref=dst, send_sem=send, recv_sem=recv,
             device_id={axis: peer}, device_id_type=MESH)
 
+    def lines_of(ref, j, g):
+        return ref.at[:, :, pl.ds(pl.multiple_of((j * gx + g) * rows, rows), rows), :]
+
     def out_x(j):
         copies = []
         for s in range(1, gx):
             peer = lax.rem(me_x + s, gx)
-            copies.append(remote(first.at[j, peer], xb.at[j, me_x],
+            copies.append(remote(lines_of(first, j, peer), xb.at[j, me_x],
                                  b_send.at[j, s - 1], b_recv.at[j, s - 1], "gx", peer))
-        mine = pltpu.make_async_copy(first.at[j, me_x], xb.at[j, me_x], own.at[0, j])
+        mine = pltpu.make_async_copy(lines_of(first, j, me_x), xb.at[j, me_x], own.at[0, j])
         return copies, mine
 
     def out_y(j):
@@ -131,9 +146,9 @@
         copies = []
         for s in range(1, gx):
             peer = lax.rem(me_x + s, gx)
-            copies.append(remote(xb.at[j, peer], ylines.at[j, me_x],
+            copies.append(remote(xb.at[j, peer], lines_of(ylines, j, me_x),
                                  f_send.at[j, s - 1], f_recv.at[j, s - 1], "gx", peer))
-        mine = pltpu.make_async_copy(xb.at[j, me_x], ylines.at[j, me_x], own.at[3, j])
+        mine = pltpu.make_async_copy(xb.at[j, me_x], lines_of(ylines, j, me_x), own.at[3, j])
         return copies, mine
 
     def start(pair):
@@ -160,10 +175,10 @@
     def forward(j):
         for h in range(2):
             for g in range(gx):
-                xs[:, g * LANES:(g + 1) * LANES] = xb[j, g, :, h].reshape(m, LANES)
+                xs[:, g * LANES:(g + 1) * LANES] = xb[j, g, h].reshape(m, LANES)
             for q in range(gx // 2):
-                even = xb[j, 2 * q, :, 2].reshape(m, LANES)
-                odd = xb[j, 2 * q + 1, :, 2].reshape(m, LANES)
+                even = xb[j, 2 * q, 2].reshape(m, LANES)
+                odd = xb[j, 2 * q + 1, 2].reshape(m, LANES)
                 low, high = (even, odd) if h == 0 else (odd, even)
                 at = whole_a + q * LANES
                 xs[:, at:at + LANES] = jnp.where(low_lanes((m, LANES)), low, high)
@@ -176,8 +191,14 @@
                               preferred_element_type=jnp.float32)
                 acc += jnp.dot(xs[:, whole_a:], xf[base:base + part_b, cols],
                                preferred_element_type=jnp.float32)
-                sec[j, :, h * comps_half:(h + 1) * comps_half, cols] = (
-                    acc.astype(jnp.bfloat16).reshape(rows, comps_half, TILE))
+                for i in range(TILE // LANES):
+                    spread[i] = acc[:, i * LANES:(i + 1) * LANES]
+                for i in range(TILE // LANES):
+                    lanes = pl.ds(pl.multiple_of(n * TILE + i * LANES, LANES), LANES)
+                    for y in range(rows):
+                        line = spread[i, pl.ds(y, comps_half, stride=rows), :]
+                        sec[j, y, h * comps_half:(h + 1) * comps_half, lanes] = (
+                            line.astype(jnp.bfloat16))
 
     def columns(j):
         @pl.loop(0, CHUNK_ROWS)
@@ -198,6 +219,12 @@
         def lines(h):
             return ret[j, :, h * comps_half:(h + 1) * comps_half, :].reshape(m, width)
 
+        def put(part, g, t, i):
+            spread[i] = part
+            for c in range(comps_half):
+                line = spread[i, pl.ds(c, rows, stride=comps_half), :]
+                xb[j, g, t, c] = line.astype(jnp.bfloat16)
+
         def dots(block, at):
             return lax.dot_general(block, xf[pl.ds(at, TILE), :], (((1,), (1,)), ((), ())),
                                    preferred_element_type=jnp.float32)
@@ -207,9 +234,7 @@
             def _(n):
                 part = dots(lines(h), pl.multiple_of(n * TILE, TILE))
                 for i in range(TILE // LANES):
-                    xb[j, n * (TILE // LANES) + i, :, h] = (
-                        part[:, i * LANES:(i + 1) * LANES].astype(jnp.bfloat16)
-                        .reshape(rows, comps_half, LANES))
+                    put(part[:, i * LANES:(i + 1) * LANES], n * (TILE // LANES) + i, h, i)
 
         @pl.loop(0, part_b // TILE)
         def _(n):
@@ -221,10 +246,8 @@
                 p1 = part1[:, i * LANES:(i + 1) * LANES]
                 mask = low_lanes((m, LANES))
                 g = 2 * (n * (TILE // LANES) + i)
-                xb[j, g, :, 2] = jnp.where(mask, p0, p1).astype(jnp.bfloat16).reshape(
-                    rows, comps_half, LANES)
-                xb[j, g + 1, :, 2] = jnp.where(mask, p1, p0).astype(jnp.bfloat16).reshape(
-                    rows, comps_half, LANES)
+                put(jnp.where(mask, p0, p1), g, 2, 0)
+                put(jnp.where(mask, p1, p0), g + 1, 2, 1)
 
     bs, ds, es, fs = {}, {}, {}, {}
 
@@ -248,9 +271,13 @@
         adjoint(j)
         fs[j] = start(back_x(j))
 
-    norm_load(0).start()
     for j in range(min(2, chunks)):
         bs[j] = start(out_x(j))
+    for copy in xf_copies:
+        copy.start()
+    norm_load(0).start()
+    for copy in xf_copies:
+        copy.wait()
     stage_c(0)
     stage_e(0)
     for j in range(1, chunks):
@@ -265,9 +292,11 @@
             drain(pair)
 
 
-def exchange(gx, gy, first, norm_field, xf, factor):
-    chunks, _, rows, _, comps_half, _ = first.shape
-    width = xf.shape[1]
+def exchange(gx, gy, first, norm_field, x_filter, factor):
+    _, comps_half, lines, _ = first.shape
+    rows = gy * CHUNK_ROWS
+    chunks = lines // (gx * rows)
+    width = x_filter.shape[1]
     dma = pltpu.SemaphoreType.DMA
     all_comps = norm_field.shape[1]
     return pl.pallas_call(
@@ -276,77 +305,112 @@
         in_specs=[
             pl.BlockSpec(memory_space=pl.ANY),
             pl.BlockSpec(memory_space=pl.ANY),
-            pl.BlockSpec(memory_space=pltpu.VMEM),
+            pl.BlockSpec(memory_space=pl.ANY),
             pl.BlockSpec(memory_space=pltpu.VMEM),
         ],
         out_specs=pl.BlockSpec(memory_space=pl.ANY),
         scratch_shapes=[
-            pltpu.VMEM(first.shape, jnp.bfloat16),
+            pltpu.VMEM((chunks, gx, 3, comps_half, rows, LANES), jnp.bfloat16),
             pltpu.VMEM((chunks, rows, 2 * comps_half, width), jnp.bfloat16),
             pltpu.VMEM((chunks, CHUNK_ROWS, all_comps, width), jnp.bfloat16),
             pltpu.VMEM((chunks, rows, 2 * comps_half, width), jnp.bfloat16),
             pltpu.VMEM((rows * comps_half, width), jnp.bfloat16),
             pltpu.VMEM((CHUNK_ROWS, all_comps, width), jnp.float32),
+            pltpu.VMEM((gx * (LANES + 2 * HALF), width), jnp.bfloat16),
+            pltpu.VMEM((TILE // LANES, rows * comps_half, LANES), jnp.float32),
             dma((chunks, gx - 1)), dma((chunks, gx - 1)),
             dma((chunks, gy - 1)), dma((chunks, gy - 1)),
             dma((chunks, gy - 1)), dma((chunks, gy - 1)),
             dma((chunks, gx - 1)), dma((chunks, gx - 1)),
-            dma((4, chunks)), dma,
+            dma((4, chunks)), dma, dma((3 * gx,)),
         ],
         compiler_params=pltpu.CompilerParams(
             collective_id=0, has_side_effects=True, vmem_limit_bytes=60 * 1024 * 1024),
         name="exchange",
-    )(first, norm_field, xf, factor)
-
-
-def pack(block, odd):
-    half = block.shape[1] // 2
-    b0, b1 = block[:, :half, LANES:], block[:, half:, LANES:]
-    tail = jnp.where(odd, jnp.concatenate([b1, b0], 2), jnp.concatenate([b0, b1], 2))
-    return jnp.concatenate([block[:, :half, :LANES], block[:, half:, :LANES], tail], 1)
-
-
-def unpack(block, odd):
-    half = block.shape[1] // 3
-    tail = block[:, 2 * half:]
-    low, high = tail[:, :, :HALF], tail[:, :, HALF:]
-    b0, b1 = jnp.where(odd, high, low), jnp.where(odd, low, high)
-    return jnp.concatenate([
-        jnp.concatenate([block[:, :half], b0], 2),
-        jnp.concatenate([block[:, half:2 * half], b1], 2)], 1)
+    )(first, norm_field, x_filter, factor)
+
+
+def first_kernel(yf, field, first):
+    odd = lax.rem(lax.axis_index("gx"), 2)
+    comps = field.shape[1]
+    parts = [field[h, c, :LANES, :] for h in range(2) for c in range(comps)]
+    for c in range(comps):
+        parts += [field[odd, c, LANES:, :], field[1 - odd, c, LANES:, :]]
+    result = lax.dot_general(yf[...], jnp.concatenate(parts, 0), (((1,), (1,)), ((), ())),
+                             preferred_element_type=jnp.float32)
+    for t in range(3):
+        for c in range(comps):
+            at = (t * comps + c) * LANES
+            first[t, c] = result[:, at:at + LANES].astype(jnp.bfloat16)
+
+
+def first_lines(yf, field):
+    _, half, strip, lines = field.shape
+    step = 2
+    return pl.pallas_call(
+        first_kernel,
+        grid=(half // step,),
+        out_shape=jax.ShapeDtypeStruct((3, half, lines, LANES), jnp.bfloat16),
+        in_specs=[
+            pl.BlockSpec((lines, lines), lambda i: (0, 0)),
+            pl.BlockSpec((2, step, strip, lines), lambda i: (0, i, 0, 0)),
+        ],
+        out_specs=pl.BlockSpec((3, step, lines, LANES), lambda i: (0, i, 0, 0)),
+        compiler_params=pltpu.CompilerParams(vmem_limit_bytes=48 * 1024 * 1024),
+        name="first_lines",
+    )(yf, field)
+
+
+def last_kernel(yf, ylines, result):
+    odd = lax.rem(lax.axis_index("gx"), 2)
+    comps = ylines.shape[1]
+    lines = jnp.concatenate(
+        [ylines[t, c] for t in range(3) for c in range(comps)], 1)
+    total = jnp.dot(lines.T, yf[...], preferred_element_type=jnp.float32).astype(jnp.bfloat16)
+    for c in range(comps):
+        for h in range(2):
+            at = (h * comps + c) * LANES
+            result[h, c, :LANES, :] = total[at:at + LANES]
+        at = (2 * comps + c) * LANES
+        result[odd, c, LANES:, :] = total[at:at + HALF]
+        result[1 - odd, c, LANES:, :] = total[at + HALF:at + LANES]
+
+
+def last_lines(yf, ylines):
+    _, half, lines, _ = ylines.shape
+    strip = LANES + HALF
+    step = 2
+    return pl.pallas_call(
+        last_kernel,
+        grid=(half // step,),
+        out_shape=jax.ShapeDtypeStruct((2, half, strip, lines), jnp.bfloat16),
+        in_specs=[
+            pl.BlockSpec((lines, lines), lambda i: (0, 0)),
+            pl.BlockSpec((3, step, lines, LANES), lambda i: (0, i, 0, 0)),
+        ],
+        out_specs=pl.BlockSpec((2, step, strip, lines), lambda i: (0, i, 0, 0)),
+        compiler_params=pltpu.CompilerParams(vmem_limit_bytes=48 * 1024 * 1024),
+        name="last_lines",
+    )(yf, ylines)
 
 
 def fused_plan(gx, gy, field, norm_field, vertical, x_filter, y_filter):
     lines, comps, width = field.shape
     chunks = norm_field.shape[0] // CHUNK_ROWS
     half = comps // 2
-    odd = lax.rem(lax.axis_index("gx"), 2) == 1
 
     product = jnp.einsum("skl,sml->skm", vertical, vertical, precision=lax.Precision.HIGHEST)
     high = lax.reduce_precision(product, 8, 7)
     low = product - high
     factor = jnp.concatenate([high, low, high], 2).astype(jnp.bfloat16)
 
-    strips = x_filter.reshape(gx, width, -1)
-    tails = strips[:, LANES:].reshape(gx // 2, 2, HALF, -1)
-    xf = jnp.concatenate([
-        strips[:, :LANES].reshape(gx * LANES, -1),
-        tails.reshape(gx * HALF, -1),
-        tails[:, ::-1].reshape(gx * HALF, -1)], 0)
-
     yf = y_filter.reshape(lines, gx, gy, chunks, CHUNK_ROWS)
-    yf = yf.transpose(0, 3, 1, 2, 4).reshape(lines, lines)
-
-    packed = pack(field, odd)
-    first = lax.dot_general(
-        yf, packed, (((0,), (0,)), ((), ())), preferred_element_type=jnp.float32)
-    first = first.astype(jnp.bfloat16).reshape(
-        chunks, gx, gy * CHUNK_ROWS, 3, half, LANES)
-    ylines = exchange(gx, gy, first, norm_field, xf, factor)
-    ylines = ylines.reshape(lines, 3 * half, LANES)
-    result = lax.dot_general(
-        yf, ylines, (((1,), (0,)), ((), ())), preferred_element_type=jnp.float32)
-    return unpack(result.astype(jnp.bfloat16), odd)
+    yf = yf.transpose(3, 1, 2, 4, 0).reshape(lines, lines)
+
+    first = first_lines(yf, field.transpose(1, 2, 0).reshape(2, half, width, lines))
+    ylines = exchange(gx, gy, first, norm_field, x_filter, factor)
+    result = last_lines(yf, ylines)
+    return result.reshape(comps, width, lines).transpose(2, 0, 1)
 
 
 def per_device(gx, gy, field, norm_field, vertical, x_filter, y_filter):

time: 496 us -> 450 us (0.907); the launches traced: 496 us -> 444 us
  matrix products: 28.5 us -> 0.24 us
  local copies, waits for them, and re-layouts: 26.4 us -> 2.53 us
  Pallas kernels: 419 us -> 440 us
  other arithmetic: 21.7 us -> 0.71 us
    dot_general x2 -> x0, matrix products: 28.2 us -> none  [the longest x1 17.1 us: fused_plan(): lax.dot_general(yf, ylines, (((1,), (0,)), ((), ())), preferred_element_t...]
    pallas_call x0 -> x2, Pallas kernels: none -> 26.7 us  [the longest x1 13.4 us: last_lines(): pl.pallas_call(last_kernel, grid=(half // step,), out_shape=jax.ShapeDtyp...]
    concatenate x2 -> x0, other arithmetic: 19.9 us -> none  [the longest x1 16.8 us: unpack(): jnp.concatenate([jnp.concatenate([block[:, :half], b0], 2), jnp.concatena...]
    convert_element_type x1 -> x0, local copies, waits for them, and re-layouts: 13.2 us -> none  [fused_plan(): first.astype(jnp.bfloat16)]
    slice x6 -> x0, local copies, waits for them, and re-layouts: 9.16 us -> none  [the longest x2 2.77 us: pack(): block[:, :half, :LANES]]
    pallas_call x1, Pallas kernels: 419 us -> 413 us  [exchange(): pl.pallas_call(functools.partial(exchange_kernel, gx, gy), out_shape=jax....]
where the time goes in v2:
time: 450 us; the launch traced here: 444 us
  Pallas kernels  440 us (98%)
    pallas_call x1, Pallas kernels, exchange(): pl.pallas_call(functools.partial(exchange_kernel, gx, gy), out_shape=jax....  413 us
    pallas_call x1, Pallas kernels, last_lines(): pl.pallas_call(last_kernel, grid=(half // step,), out_shape=jax.ShapeDtyp...  13.4 us
    pallas_call x1, Pallas kernels, first_lines(): pl.pallas_call(first_kernel, grid=(half // step,), out_shape=jax.ShapeDty...  13.3 us

profile of v2, /device:TPU:30, one launch (start us, length us, event | category | flops | bytes accessed | tf_op | source)
XLA Modules:
  0.0 443.6 jit_solution(4145505042085285264)
XLA Ops:
  0.0 0.0 copy-start
  0.0 0.8 copy-done
  0.8 0.2 fusion
  1.1 0.7 pad_maximum_fusion.factor
  1.8 1.6 copy.7
  3.4 0.1 copy.8
  3.5 13.3 %first_lines.1.first = bf16[3,16,768,128]{3,2,1,0:T(8,128)(2,1)} custom-call(bf16[768,768]{1,0:T(8,128)(2,1)S(1)} %bitcast.12, bf16[2,16,192,768]{3,2,1,0:T(8,128)(2,1)} %bitcast.14), custom_call_target="tpu_custom_call" | custom-call | tf_op jit(solution)/shard_map/first_lines/pallas_call | solution.py:350
  16.8 413.4 %exchange.1.ylines = bf16[3,16,768,128]{3,2,1,0:T(8,128)(2,1)} custom-call(bf16[3,16,768,128]{3,2,1,0:T(8,128)(2,1)} %first_lines.1.first, f32[24,128,1536]{2,1,0:T(8,128)} %norm.1, bf16[1536,1536]{1,0:T(8,128)(2,1)} %x_filter.1, bf16[2,64,192]{2,1,0:T(8,128)(2,1)} %pad_maximum_fusion.factor), custom_call_target="tpu_custom_call" | custom-call | tf_op jit(solution)/shard_map/exchange/pallas_call | solution.py:302
  430.2 13.4 %last_lines.1 = bf16[2,16,192,768]{3,2,1,0:T(8,128)(2,1)} custom-call(bf16[768,768]{1,0:T(8,128)(2,1)S(1)} %bitcast.13, bf16[3,16,768,128]{3,2,1,0:T(8,128)(2,1)} %exchange.1.ylines), custom_call_target="tpu_custom_call" | custom-call | tf_op jit(solution)/shard_map/last_lines/pallas_call | solution.py:383
Async XLA Ops:
  0.0 0.8 copy-start

commit v3 on v2

--- a/solution.py
+++ b/solution.py
@@ -10,7 +10,9 @@
 MESH = pl.DeviceIdType.MESH
 LANES = 128
 HALF = 64
-CHUNK_ROWS = 8
+CHUNK_ROWS = 4
+SLOTS = 3
+STEP = 2
 TILE = 256
 
 
@@ -64,9 +66,9 @@
 
 
 def exchange_kernel(
-    gx, gy, first, norm, x_filter, factor, ylines,
-    xb, sec, col, ret, xs, nbuf, xf, spread,
-    b_send, b_recv, d_send, d_recv, e_send, e_recv, f_send, f_recv, own, nsem, xsem,
+    gx, gy, field_in, norm, x_filter, factor, yf, ylines,
+    xb, sec, col, ret, xs, nbuf, xf, spread, field, first,
+    b_send, b_recv, d_send, d_recv, e_send, e_recv, f_send, f_recv, own, nsem, xsem, fsem,
 ):
     chunks, _, _, comps_half, rows, _ = xb.shape
     comps = 2 * comps_half
@@ -90,6 +92,14 @@
             xf_copies.append(pltpu.make_async_copy(
                 src, xf.at[pl.ds(at, src.shape[0])], xsem.at[len(xf_copies)]))
 
+    def field_load(i):
+        some = pl.ds(i * STEP, STEP)
+        return pltpu.make_async_copy(field_in.at[:, some], field.at[:, some], fsem.at[i])
+
+    @pl.loop(0, comps_half // STEP)
+    def _(i):
+        field_load(i).start()
+
     barrier = pltpu.get_barrier_semaphore()
     for s in range(1, gx):
         pl.semaphore_signal(
@@ -111,9 +121,9 @@
         copies = []
         for s in range(1, gx):
             peer = lax.rem(me_x + s, gx)
-            copies.append(remote(lines_of(first, j, peer), xb.at[j, me_x],
+            copies.append(remote(first.at[j % SLOTS, peer], xb.at[j, me_x],
                                  b_send.at[j, s - 1], b_recv.at[j, s - 1], "gx", peer))
-        mine = pltpu.make_async_copy(lines_of(first, j, me_x), xb.at[j, me_x], own.at[0, j])
+        mine = pltpu.make_async_copy(first.at[j % SLOTS, me_x], xb.at[j, me_x], own.at[0, j])
         return copies, mine
 
     def out_y(j):
@@ -121,11 +131,11 @@
         for s in range(1, gy):
             peer = lax.rem(me_y + s, gy)
             copies.append(remote(
-                sec.at[j, pl.ds(peer * CHUNK_ROWS, CHUNK_ROWS)],
+                sec.at[j % SLOTS, pl.ds(peer * CHUNK_ROWS, CHUNK_ROWS)],
                 col.at[j, :, pl.ds(pl.multiple_of(me_y * comps, comps), comps), :],
                 d_send.at[j, s - 1], d_recv.at[j, s - 1], "gy", peer))
         mine = pltpu.make_async_copy(
-            sec.at[j, pl.ds(me_y * CHUNK_ROWS, CHUNK_ROWS)],
+            sec.at[j % SLOTS, pl.ds(me_y * CHUNK_ROWS, CHUNK_ROWS)],
             col.at[j, :, pl.ds(pl.multiple_of(me_y * comps, comps), comps), :], own.at[1, j])
         return copies, mine
 
@@ -168,6 +178,27 @@
 
     def norm_load(j):
         return pltpu.make_async_copy(norm.at[pl.ds(j * CHUNK_ROWS, CHUNK_ROWS)], nbuf, nsem)
+
+    odd = lax.rem(me_x, 2)
+
+    def first_lines(j):
+        @pl.loop(0, comps_half // STEP)
+        def _(i):
+            if j == 0:
+                field_load(i).wait()
+            cs = [i * STEP + c for c in range(STEP)]
+            parts = [field[h, c, :LANES, :] for h in range(2) for c in cs]
+            for c in cs:
+                parts += [field[odd, c, LANES:, :], field[1 - odd, c, LANES:, :]]
+            result = lax.dot_general(
+                yf[j * gx * rows:(j + 1) * gx * rows, :], jnp.concatenate(parts, 0),
+                (((1,), (1,)), ((), ())), preferred_element_type=jnp.float32)
+            for t in range(3):
+                for c in range(STEP):
+                    at = (t * STEP + c) * LANES
+                    lines = result[:, at:at + LANES].astype(jnp.bfloat16)
+                    for g in range(gx):
+                        first[j % SLOTS, g, t, cs[c]] = lines[g * rows:(g + 1) * rows]
 
     def low_lanes(shape):
         return lax.broadcasted_iota(jnp.int32, shape, len(shape) - 1) < HALF
@@ -197,7 +228,7 @@
                     lanes = pl.ds(pl.multiple_of(n * TILE + i * LANES, LANES), LANES)
                     for y in range(rows):
                         line = spread[i, pl.ds(y, comps_half, stride=rows), :]
-                        sec[j, y, h * comps_half:(h + 1) * comps_half, lanes] = (
+                        sec[j % SLOTS, y, h * comps_half:(h + 1) * comps_half, lanes] = (
                             line.astype(jnp.bfloat16))
 
     def columns(j):
@@ -253,10 +284,14 @@
 
     def stage_c(j):
         arrive(bs[j])
-        if j + 2 < chunks:
-            bs[j + 2] = start(out_x(j + 2))
+        if j >= SLOTS:
+            drain(ds[j - SLOTS])
         forward(j)
         ds[j] = start(out_y(j))
+        if j + SLOTS < chunks:
+            drain(bs[j])
+            first_lines(j + SLOTS)
+            bs[j + SLOTS] = start(out_x(j + SLOTS))
 
     def stage_e(j):
         arrive(ds[j])
@@ -271,7 +306,8 @@
         adjoint(j)
         fs[j] = start(back_x(j))
 
-    for j in range(min(2, chunks)):
+    for j in range(min(SLOTS, chunks)):
+        first_lines(j)
         bs[j] = start(out_x(j))
     for copy in xf_copies:
         copy.start()
@@ -288,12 +324,13 @@
     for j in range(chunks):
         arrive(fs[j])
     for j in range(chunks):
-        for pair in (bs[j], ds[j], es[j], fs[j]):
-            drain(pair)
-
-
-def exchange(gx, gy, first, norm_field, x_filter, factor):
-    _, comps_half, lines, _ = first.shape
+        for pair, slots in ((bs[j], SLOTS), (ds[j], SLOTS), (es[j], 0), (fs[j], 0)):
+            if j + slots >= chunks or slots == 0:
+                drain(pair)
+
+
+def exchange(gx, gy, field, norm_field, x_filter, factor, yf):
+    _, comps_half, strip, lines = field.shape
     rows = gy * CHUNK_ROWS
     chunks = lines // (gx * rows)
     width = x_filter.shape[1]
@@ -301,64 +338,36 @@
     all_comps = norm_field.shape[1]
     return pl.pallas_call(
         functools.partial(exchange_kernel, gx, gy),
-        out_shape=jax.ShapeDtypeStruct(first.shape, jnp.bfloat16),
+        out_shape=jax.ShapeDtypeStruct((3, comps_half, lines, LANES), jnp.bfloat16),
         in_specs=[
             pl.BlockSpec(memory_space=pl.ANY),
             pl.BlockSpec(memory_space=pl.ANY),
             pl.BlockSpec(memory_space=pl.ANY),
             pl.BlockSpec(memory_space=pltpu.VMEM),
+            pl.BlockSpec(memory_space=pltpu.VMEM),
         ],
         out_specs=pl.BlockSpec(memory_space=pl.ANY),
         scratch_shapes=[
             pltpu.VMEM((chunks, gx, 3, comps_half, rows, LANES), jnp.bfloat16),
-            pltpu.VMEM((chunks, rows, 2 * comps_half, width), jnp.bfloat16),
+            pltpu.VMEM((SLOTS, rows, 2 * comps_half, width), jnp.bfloat16),
             pltpu.VMEM((chunks, CHUNK_ROWS, all_comps, width), jnp.bfloat16),
             pltpu.VMEM((chunks, rows, 2 * comps_half, width), jnp.bfloat16),
             pltpu.VMEM((rows * comps_half, width), jnp.bfloat16),
             pltpu.VMEM((CHUNK_ROWS, all_comps, width), jnp.float32),
             pltpu.VMEM((gx * (LANES + 2 * HALF), width), jnp.bfloat16),
             pltpu.VMEM((TILE // LANES, rows * comps_half, LANES), jnp.float32),
+            pltpu.VMEM(field.shape, jnp.bfloat16),
+            pltpu.VMEM((SLOTS, gx, 3, comps_half, rows, LANES), jnp.bfloat16),
             dma((chunks, gx - 1)), dma((chunks, gx - 1)),
             dma((chunks, gy - 1)), dma((chunks, gy - 1)),
             dma((chunks, gy - 1)), dma((chunks, gy - 1)),
             dma((chunks, gx - 1)), dma((chunks, gx - 1)),
-            dma((4, chunks)), dma, dma((3 * gx,)),
+            dma((4, chunks)), dma, dma((3 * gx,)), dma((comps_half // STEP,)),
         ],
         compiler_params=pltpu.CompilerParams(
             collective_id=0, has_side_effects=True, vmem_limit_bytes=60 * 1024 * 1024),
         name="exchange",
-    )(first, norm_field, x_filter, factor)
-
-
-def first_kernel(yf, field, first):
-    odd = lax.rem(lax.axis_index("gx"), 2)
-    comps = field.shape[1]
-    parts = [field[h, c, :LANES, :] for h in range(2) for c in range(comps)]
-    for c in range(comps):
-        parts += [field[odd, c, LANES:, :], field[1 - odd, c, LANES:, :]]
-    result = lax.dot_general(yf[...], jnp.concatenate(parts, 0), (((1,), (1,)), ((), ())),
-                             preferred_element_type=jnp.float32)
-    for t in range(3):
-        for c in range(comps):
-            at = (t * comps + c) * LANES
-            first[t, c] = result[:, at:at + LANES].astype(jnp.bfloat16)
-
-
-def first_lines(yf, field):
-    _, half, strip, lines = field.shape
-    step = 2
-    return pl.pallas_call(
-        first_kernel,
-        grid=(half // step,),
-        out_shape=jax.ShapeDtypeStruct((3, half, lines, LANES), jnp.bfloat16),
-        in_specs=[
-            pl.BlockSpec((lines, lines), lambda i: (0, 0)),
-            pl.BlockSpec((2, step, strip, lines), lambda i: (0, i, 0, 0)),
-        ],
-        out_specs=pl.BlockSpec((3, step, lines, LANES), lambda i: (0, i, 0, 0)),
-        compiler_params=pltpu.CompilerParams(vmem_limit_bytes=48 * 1024 * 1024),
-        name="first_lines",
-    )(yf, field)
+    )(field, norm_field, x_filter, factor, yf)
 
 
 def last_kernel(yf, ylines, result):
@@ -379,7 +388,7 @@
 def last_lines(yf, ylines):
     _, half, lines, _ = ylines.shape
     strip = LANES + HALF
-    step = 2
+    step = STEP
     return pl.pallas_call(
         last_kernel,
         grid=(half // step,),
@@ -407,8 +416,8 @@
     yf = y_filter.reshape(lines, gx, gy, chunks, CHUNK_ROWS)
     yf = yf.transpose(3, 1, 2, 4, 0).reshape(lines, lines)
 
-    first = first_lines(yf, field.transpose(1, 2, 0).reshape(2, half, width, lines))
-    ylines = exchange(gx, gy, first, norm_field, x_filter, factor)
+    strips = field.transpose(1, 2, 0).reshape(2, half, width, lines)
+    ylines = exchange(gx, gy, strips, norm_field, x_filter, factor, yf)
     result = last_lines(yf, ylines)
     return result.reshape(comps, width, lines).transpose(2, 0, 1)
 
@@ -417,7 +426,7 @@
     lines, comps, width = field.shape
     rows, all_comps, whole = norm_field.shape
     fits = (
-        width == LANES + HALF and comps == 32 and rows % CHUNK_ROWS == 0 and gx % 4 == 0
+        width == LANES + HALF and comps == 32 and rows % CHUNK_ROWS == 0 and gy * CHUNK_ROWS % 16 == 0 and gx % 4 == 0
         and gy > 1 and whole % (2 * TILE) == 0 and vertical.shape[1] % 16 == 0
         and rows * all_comps * whole <= 24 * 128 * 1536
     )

time: 450 us -> 441 us (0.980); the launches traced: 444 us -> 440 us
  Pallas kernels: 440 us -> 434 us
    pallas_call x1 -> x0, Pallas kernels: 13.3 us -> none  [first_lines(): pl.pallas_call(first_kernel, grid=(half // step,), out_shape=jax.ShapeDty...]
    pallas_call x1, Pallas kernels: 413 us -> 421 us  [exchange(): pl.pallas_call(functools.partial(exchange_kernel, gx, gy), out_shape=jax....]
where the time goes in v3:
time: 441 us; the launch traced here: 440 us
  Pallas kernels  434 us (98%)
    pallas_call x1, Pallas kernels, exchange(): pl.pallas_call(functools.partial(exchange_kernel, gx, gy), out_shape=jax....  421 us
    pallas_call x1, Pallas kernels, last_lines(): pl.pallas_call(last_kernel, grid=(half // step,), out_shape=jax.ShapeDtyp...  13.4 us

profile of v3, /device:TPU:30, one launch (start us, length us, event | category | flops | bytes accessed | tf_op | source)
XLA Modules:
  0.0 439.8 jit_solution(3314496792900380372)
XLA Ops:
  0.0 0.0 copy-start
  0.0 0.8 copy-done
  0.8 0.2 fusion
  1.1 0.7 pad_maximum_fusion.factor
  1.8 1.6 copy.7
  3.4 0.3 reshape.12
  3.7 0.4 copy.8
  4.1 1.2 reshape.13.yf
  5.3 0.0 copy-start.1
  5.3 421.1 %exchange.1.ylines = bf16[3,16,768,128]{3,2,1,0:T(8,128)(2,1)} custom-call(bf16[2,16,192,768]{3,2,1,0:T(8,128)(2,1)} %bitcast.11, f32[24,128,1536]{2,1,0:T(8,128)} %norm.1, bf16[1536,1536]{1,0:T(8,128)(2,1)} %x_filter.1, bf16[2,64,192]{2,1,0:T(8,128)(2,1)} %pad_maximum_fusion.factor, bf16[768,768]{1,0:T(8,128)(2,1)} %reshape.13.yf), custom_call_target="tpu_custom_call" | custom-call | tf_op jit(solution)/shard_map/exchange/pallas_call | solution.py:339
  426.4 0.0 copy-done.1
  426.4 13.4 %last_lines.1 = bf16[2,16,192,768]{3,2,1,0:T(8,128)(2,1)} custom-call(bf16[768,768]{1,0:T(8,128)(2,1)S(1)} %copy-done.1, bf16[3,16,768,128]{3,2,1,0:T(8,128)(2,1)} %exchange.1.ylines), custom_call_target="tpu_custom_call" | custom-call | tf_op jit(solution)/shard_map/last_lines/pallas_call | solution.py:392
Async XLA Ops:
  0.0 0.8 copy-start
  5.3 421.1 %copy-start.1 = (bf16[768,768]{1,0:T(8,128)(2,1)S(1)}, bf16[768,768]{1,0:T(8,128)(2,1)}, u32[]{:S(2)}) copy-start(bf16[768,768]{1,0:T(8,128)(2,1)} %reshape.13.yf) | copy-start | bytes 3538948

commit v4 on v3

--- a/solution.py
+++ b/solution.py
@@ -13,6 +13,7 @@
 CHUNK_ROWS = 4
 SLOTS = 3
 STEP = 2
+LAG = 3
 TILE = 256
 
 
@@ -314,13 +315,13 @@
     norm_load(0).start()
     for copy in xf_copies:
         copy.wait()
-    stage_c(0)
-    stage_e(0)
-    for j in range(1, chunks):
-        stage_c(j)
-        stage_f(j - 1)
-        stage_e(j)
-    stage_f(chunks - 1)
+    for j in range(chunks + LAG):
+        if j < chunks:
+            stage_c(j)
+        if 1 <= j <= chunks:
+            stage_e(j - 1)
+        if j >= LAG:
+            stage_f(j - LAG)
     for j in range(chunks):
         arrive(fs[j])
     for j in range(chunks):

time: 441 us -> 441 us (level)
  no operation moved by 1% of the time
where the time goes in v4:
time: 441 us; the launch traced here: 438 us
  Pallas kernels  432 us (98%)
    pallas_call x1, Pallas kernels, exchange(): pl.pallas_call(functools.partial(exchange_kernel, gx, gy), out_shape=jax....  419 us
    pallas_call x1, Pallas kernels, last_lines(): pl.pallas_call(last_kernel, grid=(half // step,), out_shape=jax.ShapeDtyp...  13.4 us

profile of v4, /device:TPU:30, one launch (start us, length us, event | category | flops | bytes accessed | tf_op | source)
XLA Modules:
  0.0 437.5 jit_solution(1762207123513870858)
XLA Ops:
  0.0 0.0 copy-start
  0.0 0.8 copy-done
  0.8 0.2 fusion
  1.1 0.7 pad_maximum_fusion.factor
  1.8 1.6 copy.7
  3.4 0.3 reshape.12
  3.7 0.4 copy.8
  4.1 1.2 reshape.13.yf
  5.3 0.0 copy-start.1
  5.3 418.8 %exchange.1.ylines = bf16[3,16,768,128]{3,2,1,0:T(8,128)(2,1)} custom-call(bf16[2,16,192,768]{3,2,1,0:T(8,128)(2,1)} %bitcast.11, f32[24,128,1536]{2,1,0:T(8,128)} %norm.1, bf16[1536,1536]{1,0:T(8,128)(2,1)} %x_filter.1, bf16[2,64,192]{2,1,0:T(8,128)(2,1)} %pad_maximum_fusion.factor, bf16[768,768]{1,0:T(8,128)(2,1)} %reshape.13.yf), custom_call_target="tpu_custom_call" | custom-call | tf_op jit(solution)/shard_map/exchange/pallas_call | solution.py:340
  424.1 0.0 copy-done.1
  424.2 13.4 %last_lines.1 = bf16[2,16,192,768]{3,2,1,0:T(8,128)(2,1)} custom-call(bf16[768,768]{1,0:T(8,128)(2,1)S(1)} %copy-done.1, bf16[3,16,768,128]{3,2,1,0:T(8,128)(2,1)} %exchange.1.ylines), custom_call_target="tpu_custom_call" | custom-call | tf_op jit(solution)/shard_map/last_lines/pallas_call | solution.py:393
Async XLA Ops:
  0.0 0.8 copy-start
  5.3 418.8 %copy-start.1 = (bf16[768,768]{1,0:T(8,128)(2,1)S(1)}, bf16[768,768]{1,0:T(8,128)(2,1)}, u32[]{:S(2)}) copy-start(bf16[768,768]{1,0:T(8,128)(2,1)} %reshape.13.yf) | copy-start | bytes 3538948
